TPU v7x, 32 devices: a whole 2x2x4 slice. The times are simulated.
32 devices in a mesh: head: 8 (over z, y), query: 4 (over x, core).
Axes of the slice: x: 2, y: 2, z: 4, core: 2. Of those that a mesh axis runs over, the one named last changes fastest.
Arguments:
- queries: bfloat16 [4096, 32, 128], P(('query', 'head')), may hold values from -100 to 100
- keys: bfloat16 [4096, 4, 128], P(('query', 'head')), may hold values from -4 to 4
- values: bfloat16 [4096, 4, 128], P(('query', 'head')), may hold values from -6 to 6
- attention_out: bfloat16 [4096, 32, 128], P(('query', 'head')), may hold values from -3 to 3
- out_grad: bfloat16 [4096, 32, 128], P(('query', 'head')), may hold values from -6 to 6
- span_order: int32 [4, 2], replicated, may hold values from 0 to 7, as said below
- doc_lengths: int32 [16], replicated, may hold values from 1 to 512, 4096 in all
Outputs:
- query_grad: bfloat16 [4096, 32, 128], P(('query', 'head'))
- key_grad: bfloat16 [4096, 4, 128], P(('query', 'head'))
- value_grad: bfloat16 [4096, 4, 128], P(('query', 'head'))
Inputs may be any that keep to these rules, and one draw needn't show every extreme that they name: `span_order`: every number from 0 to 7 appears exactly once; the two numbers of a row sum to 7, in either order. `doc_lengths`: the lengths sum to 4096.
All inputs are finite; a program needn't handle non-finite values.
Results may differ from a plain program's by a relative error of at most 0.0058.
Values may be sent and summed in bfloat16 or wider, within the bound.
A program may use at most 128 MiB of HBM per device.

v0:
```python
import jax
import jax.numpy as jnp
from jax import lax
from jax.sharding import PartitionSpec as P

key_block = 512
masked = -1e30


def positions(span_order, doc_lengths, rows_each):
    span_rows = rows_each // 2
    within = jnp.arange(span_rows, dtype=jnp.int32)
    pos_all = (span_order[:, :, None] * span_rows + within[None, None, :]).reshape(-1)
    doc_ends = jnp.cumsum(doc_lengths)[:-1]
    doc_all = jnp.sum((pos_all[:, None] >= doc_ends[None, :]).astype(jnp.int32), axis=1)
    return (pos_all, doc_all)


def visible(pos_query, doc_query, pos_key, doc_key):
    return (pos_key[None, :] <= pos_query[:, None]) & (doc_key[None, :] == doc_query[:, None])


def skipping(pos_query, doc_query, pos_key, doc_key, compute, totals):
    maybe = jnp.any(
        (pos_query >= jnp.min(pos_key))
        & (doc_query >= jnp.min(doc_key))
        & (doc_query <= jnp.max(doc_key))
    )
    return lax.cond(maybe, compute, lambda running: running, totals)


def tile_scores(query_tile, key_tile, allowed):
    factor = query_tile.shape[-1] ** (-0.5)
    scores = (
        jnp.einsum("rkgd,ckd->kgrc", query_tile, key_tile, preferred_element_type=jnp.float32)
        * factor
    )
    return jnp.where(allowed, scores, masked)


def tile_grads(query_tile, grad_tile, key_tile, value_tile, allowed, log_rows, delta_rows):
    scores = tile_scores(query_tile, key_tile, allowed)
    probability = jnp.where(allowed, jnp.exp(scores - log_rows[..., None]), 0.0)
    grad_prob = jnp.einsum(
        "rkgd,ckd->kgrc", grad_tile, value_tile, preferred_element_type=jnp.float32
    )
    grad_score = (probability * (grad_prob - delta_rows[..., None])).astype(jnp.bfloat16)
    return (probability, grad_score)


def blockwise(totals, pieces, update):
    length = pieces[0].shape[0]

    def advance(number, running):
        row_start = number * key_block
        sliced = tuple(
            (lax.dynamic_slice_in_dim(member, row_start, key_block, 0) for member in pieces)
        )
        return update(running, sliced, row_start)

    return lax.fori_loop(0, length // key_block, advance, totals)


def shards(queries, keys, values, attention_out, out_grad, span_order, doc_lengths):
    head_count = lax.axis_size("head")
    head_copies = max(head_count // keys.shape[1], 1)
    keys_wide = jnp.repeat(keys, head_copies, axis=1)
    values_wide = jnp.repeat(values, head_copies, axis=1)
    delta_tokens = jnp.sum(
        attention_out.astype(jnp.float32) * out_grad.astype(jnp.float32), axis=-1
    )
    query_here, grad_here, key_here, value_here = (
        lax.all_to_all(queries, "head", split_axis=1, concat_axis=0, tiled=True),
        lax.all_to_all(out_grad, "head", split_axis=1, concat_axis=0, tiled=True),
        lax.all_to_all(keys_wide, "head", split_axis=1, concat_axis=0, tiled=True),
        lax.all_to_all(values_wide, "head", split_axis=1, concat_axis=0, tiled=True),
    )
    delta_here = lax.all_to_all(delta_tokens, "head", split_axis=1, concat_axis=0, tiled=True)
    rows_each, local_heads, head_dim = query_here.shape
    kv_here = key_here.shape[1]
    group_here = local_heads // kv_here
    query_here = query_here.reshape(rows_each, kv_here, group_here, head_dim)
    grad_here = grad_here.reshape(rows_each, kv_here, group_here, head_dim)
    delta = jnp.transpose(delta_here.reshape(rows_each, kv_here, group_here), (1, 2, 0))
    factor = head_dim ** (-0.5)
    pos_all, doc_all = positions(span_order, doc_lengths, rows_each)
    row_first = lax.axis_index("query") * rows_each
    pos_query = lax.dynamic_slice_in_dim(pos_all, row_first, rows_each)
    doc_query = lax.dynamic_slice_in_dim(doc_all, row_first, rows_each)
    stat_shape = (kv_here, group_here, rows_each)

    def key_place(offset, length):
        return (
            lax.dynamic_slice_in_dim(pos_all, offset, length),
            lax.dynamic_slice_in_dim(doc_all, offset, length),
        )

    start_max = jnp.full(stat_shape, masked, jnp.float32)
    start_sum = jnp.zeros(stat_shape, jnp.float32)

    def max_update(totals, pieces, offset):
        key_piece = pieces[0]
        pos_key, doc_key = key_place(offset, key_piece.shape[0])

        def compute(running):
            row_max, row_sum = running
            allowed = visible(pos_query, doc_query, pos_key, doc_key)
            scores = tile_scores(query_here, key_piece, allowed)
            new_max = jnp.maximum(row_max, jnp.max(scores, axis=-1))
            exp_scores = jnp.where(allowed, jnp.exp(scores - new_max[..., None]), 0.0)
            return (new_max, row_sum * jnp.exp(row_max - new_max) + jnp.sum(exp_scores, axis=-1))

        return skipping(pos_query, doc_query, pos_key, doc_key, compute, totals)

    row_max, row_sum = blockwise(
        (start_max, start_sum), (lax.all_gather(key_here, "query", axis=0, tiled=True),), max_update
    )
    log_sum = row_max + jnp.log(row_sum)
    query_zero = jnp.zeros((rows_each, kv_here, group_here, head_dim), jnp.float32)

    def both_update(totals, pieces, offset):
        key_piece, value_piece = (pieces[0], pieces[1])
        length = key_piece.shape[0]
        pos_key, doc_key = key_place(offset, length)

        def compute(running):
            query_sum, key_full, value_full = running
            allowed = visible(pos_query, doc_query, pos_key, doc_key)
            probability, grad_score = tile_grads(
                query_here, grad_here, key_piece, value_piece, allowed, log_sum, delta
            )
            query_sum = (
                query_sum
                + jnp.einsum(
                    "kgrc,ckd->rkgd", grad_score, key_piece, preferred_element_type=jnp.float32
                )
                * factor
            )
            key_term = (
                jnp.einsum(
                    "kgrc,rkgd->ckd", grad_score, query_here, preferred_element_type=jnp.float32
                )
                * factor
            )
            value_term = jnp.einsum(
                "kgrc,rkgd->ckd",
                probability.astype(jnp.bfloat16),
                grad_here,
                preferred_element_type=jnp.float32,
            )
            key_full = lax.dynamic_update_slice_in_dim(
                key_full,
                lax.dynamic_slice_in_dim(key_full, offset, length, 0) + key_term,
                offset,
                0,
            )
            value_full = lax.dynamic_update_slice_in_dim(
                value_full,
                lax.dynamic_slice_in_dim(value_full, offset, length, 0) + value_term,
                offset,
                0,
            )
            return (query_sum, key_full, value_full)

        return skipping(pos_query, doc_query, pos_key, doc_key, compute, totals)

    full_zero = jnp.zeros((pos_all.shape[0], kv_here, head_dim), jnp.float32)
    query_acc, key_full, value_full = blockwise(
        (query_zero, full_zero, full_zero),
        (
            lax.all_gather(key_here, "query", axis=0, tiled=True),
            lax.all_gather(value_here, "query", axis=0, tiled=True),
        ),
        both_update,
    )
    key_acc, value_acc = (
        lax.psum_scatter(key_full, "query", scatter_dimension=0, tiled=True),
        lax.psum_scatter(value_full, "query", scatter_dimension=0, tiled=True),
    )
    query_low = query_acc.reshape(rows_each, local_heads, head_dim).astype(jnp.bfloat16)
    query_rows, key_rows, value_rows = (
        lax.all_to_all(query_low, "head", split_axis=0, concat_axis=1, tiled=True),
        lax.all_to_all(
            key_acc.astype(jnp.bfloat16), "head", split_axis=0, concat_axis=1, tiled=True
        ),
        lax.all_to_all(
            value_acc.astype(jnp.bfloat16), "head", split_axis=0, concat_axis=1, tiled=True
        ),
    )
    row_count = key_rows.shape[0]
    key_grad = (
        key_rows.astype(jnp.float32)
        .reshape(row_count, -1, head_copies, head_dim)
        .sum(axis=2)
        .astype(jnp.bfloat16)
    )
    value_grad = (
        value_rows.astype(jnp.float32)
        .reshape(row_count, -1, head_copies, head_dim)
        .sum(axis=2)
        .astype(jnp.bfloat16)
    )
    return (query_rows, key_grad, value_grad)


def solution(mesh):
    return jax.shard_map(
        shards,
        mesh=mesh,
        in_specs=(
            P(("query", "head"), None, None),
            P(("query", "head"), None, None),
            P(("query", "head"), None, None),
            P(("query", "head"), None, None),
            P(("query", "head"), None, None),
            P(),
            P(),
        ),
        out_specs=(
            P(("query", "head"), None, None),
            P(("query", "head"), None, None),
            P(("query", "head"), None, None),
        ),
        check_vma=False,
    )
```

profile of v0, /device:TPU:0, one launch (start us, length us, event | category | flops | bytes accessed | tf_op | source)
XLA Modules:
  0.0 347.8 jit_solution(11585522563554537927)
XLA Ops:
  8.9 7.3 %all-to-all-start = ((bf16[128,8,128]{2,0,1:T(8,128)(2,1)}), bf16[128,8,128]{2,0,1:T(8,128)(2,1)S(1)}, u32[]{:S(2)}, u32[]{:S(2)}) async-start(bf16[128,8,128]{2,0,1:T(8,128)(2,1)} %bitcast.34), calls=%async_computation | async-start | bytes 524288 | tf_op jit(solution)/shard_map/all_to_all | solution.py:75
  17.1 8.0 %all-to-all-done = bf16[128,8,128]{2,0,1:T(8,128)(2,1)S(1)} async-done(((bf16[128,8,128]{2,0,1:T(8,128)(2,1)}), bf16[128,8,128]{2,0,1:T(8,128)(2,1)S(1)}, u32[]{:S(2)}, u32[]{:S(2)}) %all-to-all-start) | async-done | bytes 262176 | tf_op jit(solution)/shard_map/all_to_all | solution.py:75
  25.9 3.6 %all-to-all-start.2 = ((bf16[128,8,128]{2,0,1:T(8,128)(2,1)}), bf16[128,8,128]{2,0,1:T(8,128)(2,1)S(1)}, u32[]{:S(2)}, u32[]{:S(2)}) async-start(bf16[128,8,128]{2,0,1:T(8,128)(2,1)} %bitcast.41), calls=%async_computation.2 | async-start | bytes 524288 | tf_op jit(solution)/shard_map/all_to_all | solution.py:76
  32.2 5.9 %all-to-all-done.2 = bf16[128,8,128]{2,0,1:T(8,128)(2,1)S(1)} async-done(((bf16[128,8,128]{2,0,1:T(8,128)(2,1)}), bf16[128,8,128]{2,0,1:T(8,128)(2,1)S(1)}, u32[]{:S(2)}, u32[]{:S(2)}) %all-to-all-start.2) | async-done | bytes 262176 | tf_op jit(solution)/shard_map/all_to_all | solution.py:76
  38.1 3.6 %all-to-all-start.1 = ((bf16[128,32,128]{2,0,1:T(8,128)(2,1)}), bf16[128,32,128]{2,0,1:T(8,128)(2,1)S(1)}, u32[]{:S(2)}, u32[]{:S(2)}) async-start(bf16[128,32,128]{2,0,1:T(8,128)(2,1)} %copy.84), calls=%async_computation.1 | async-start | bytes 2097152 | tf_op jit(solution)/shard_map/all_to_all | solution.py:73
  43.1 24.1 %all-to-all-done.1 = bf16[128,32,128]{2,0,1:T(8,128)(2,1)S(1)} async-done(((bf16[128,32,128]{2,0,1:T(8,128)(2,1)}), bf16[128,32,128]{2,0,1:T(8,128)(2,1)S(1)}, u32[]{:S(2)}, u32[]{:S(2)}) %all-to-all-start.1) | async-done | bytes 1048608 | tf_op jit(solution)/shard_map/all_to_all | solution.py:73
  67.2 3.6 %all-to-all-start.3 = ((bf16[128,32,128]{2,0,1:T(8,128)(2,1)}), bf16[128,32,128]{2,0,1:T(8,128)(2,1)S(1)}, u32[]{:S(2)}, u32[]{:S(2)}) async-start(bf16[128,32,128]{2,0,1:T(8,128)(2,1)} %copy.87), calls=%async_computation.3 | async-start | bytes 2097152 | tf_op jit(solution)/shard_map/all_to_all | solution.py:74
  74.9 21.6 %all-to-all-done.3 = bf16[128,32,128]{2,0,1:T(8,128)(2,1)S(1)} async-done(((bf16[128,32,128]{2,0,1:T(8,128)(2,1)}), bf16[128,32,128]{2,0,1:T(8,128)(2,1)S(1)}, u32[]{:S(2)}, u32[]{:S(2)}) %all-to-all-start.3) | async-done | bytes 1048608 | tf_op jit(solution)/shard_map/all_to_all | solution.py:74
  96.5 3.6 %all-to-all-start.4 = ((f32[128,8,4]{0,2,1:T(4,128)}), f32[128,8,4]{0,2,1:T(4,128)S(1)}, u32[]{:S(2)}, u32[]{:S(2)}) async-start(f32[128,8,4]{0,2,1:T(4,128)} %bitcast.48), calls=%async_computation.4 | async-start | bytes 32768 | tf_op jit(solution)/shard_map/all_to_all | solution.py:78
  101.2 47.6 %while.32 = (s32[]{:T(128)}, f32[1,4,1024]{2,1,0:T(4,128)S(1)}, f32[1,4,1024]{2,1,0:T(4,128)S(1)}, s32[4096]{0:T(1024)S(1)}, s32[1024]{0:T(1024)S(1)}, /*index=5...) while((s32[]{:T(128)}, f32[1,4,1024]{2,1,0:T(4,128)S(1)}, ...), condition=%wide.region_11.12_spmd, body=%wide.region_2.11_spmd.sunk | while | flops 555236864 | bytes 19772220 | solution.py:61
  105.4 5.2 %conditional.4 = ((f32[1,4,1024]{2,1,0:T(4,128)S(1)}, f32[1,4,1024]{2,1,0:T(4,128)S(1)})) conditional(s32[]{:T(128)} %convert_element_type.79, (f32[1,4,1024]{2,1,0:T(4,128)S(1)}, f32[1,4,1024]{2,1,0:T(4,128)S(1)}) %tuple.96, (s32[512]{0:T(512)S(1)}, s32[1024]{0:T(1024)S(1)}, s32[512]{0:T(512)S(1)}, s32[1024]{0:T(1024)S(1)}, ...), branch_computations={%region_7.7_spmd, %region_8.0_spmd} | conditional | flops 555229184 | bytes 19755544 | solution.py:29
  114.6 5.2 %conditional.4 = ((f32[1,4,1024]{2,1,0:T(4,128)S(1)}, f32[1,4,1024]{2,1,0:T(4,128)S(1)})) conditional(s32[]{:T(128)} %convert_element_type.79, (f32[1,4,1024]{2,1,0:T(4,128)S(1)}, f32[1,4,1024]{2,1,0:T(4,128)S(1)}) %tuple.96, (s32[512]{0:T(512)S(1)}, s32[1024]{0:T(1024)S(1)}, s32[512]{0:T(512)S(1)}, s32[1024]{0:T(1024)S(1)}, ...), branch_computations={%region_7.7_spmd, %region_8.0_spmd} | conditional | flops 555229184 | bytes 19755544 | solution.py:29
  135.6 5.2 %conditional.4 = ((f32[1,4,1024]{2,1,0:T(4,128)S(1)}, f32[1,4,1024]{2,1,0:T(4,128)S(1)})) conditional(s32[]{:T(128)} %convert_element_type.79, (f32[1,4,1024]{2,1,0:T(4,128)S(1)}, f32[1,4,1024]{2,1,0:T(4,128)S(1)}) %tuple.96, (s32[512]{0:T(512)S(1)}, s32[1024]{0:T(1024)S(1)}, s32[512]{0:T(512)S(1)}, s32[1024]{0:T(1024)S(1)}, ...), branch_computations={%region_7.7_spmd, %region_8.0_spmd} | conditional | flops 555229184 | bytes 19755544 | solution.py:29
  152.0 80.7 %while.33 = (s32[]{:T(128)}, f32[1024,1,4,128]{0,3,2,1:T(8,128)S(1)}, f32[4096,1,128]{2,0,1:T(8,128)}, f32[4096,1,128]{2,0,1:T(8,128)}, s32[4096]{0:T(1024)S(1)}...) while((s32[]{:T(128)}, ...), condition=%wide.region_20.21_spmd, body=%wide.region_13.20_spmd.sunk | while | flops 2712346112 | bytes 53426152 | solution.py:61
  156.0 16.4 %conditional.5 = ((f32[1024,1,4,128]{0,3,2,1:T(8,128)S(1)}, f32[4096,1,128]{2,0,1:T(8,128)}, f32[4096,1,128]{2,0,1:T(8,128)})) conditional(s32[]{:T(128)} %convert_element_type.80, (f32[1024,1,4,128]{0,3,2,1:T(8,128)S(1)}, f32[4096,1,128]{2,0,1:T(8,128)}, f32[4096,1,128]{2,0,1:T(8,128)}) %tuple.100, (bf16[4096,1,128]{2,0,1:T(8,128)(2,1)}, ...), branch_computations={%region_18.18_spmd, %region_19.19_spmd} | conditional | flops 2712338432 | bytes 53409380 | solution.py:29
  158.8 4.4 %fusion.25 = f32[4096,1,128]{2,0,1:T(8,128)} fusion(f32[4096,1,128]{2,0,1:T(8,128)} %get-tuple-element.548, s32[]{:T(128)S(6)} %select_n.47, f32[512,1024,4]{1,0,2:T(8,128)S(1)} %fusion.33, f32[4,1024]{1,0:T(4,128)S(1)} %bitcast.194, pred[1024,512]{0,1:T(8,128)(4,1)S(1)} %compare_and_fusion.1, bf16[1024,1,4,128]{3,0,2,1:T(8,128)(2,1)S(1)} %copy-done.1), kind=kOutput, calls=%fused_computation.31 | convolution fusion | flops 547422208 | bytes 10502148 | tf_op jit(solution)/shard_map/while/body/eval_jaxpr/cond/branch_1_fun/kgrc,rkgd->ckd/dot_general | solution.py:145
  163.2 4.3 %fusion.13 = bf16[4,1024,512]{1,2,0:T(8,128)(2,1)S(1)} fusion(f32[512,1024,4]{1,0,2:T(8,128)S(1)} %fusion.33, f32[4,1024]{1,0:T(4,128)S(1)} %bitcast.197, f32[4,1024]{1,0:T(4,128)S(1)} %bitcast.195, pred[1024,512]{0,1:T(8,128)(4,1)S(1)} %compare_and_fusion.1, bf16[1024,1,4,128]{3,0,2,1:T(8,128)(2,1)S(1)} %copy-done.1, ...), kind=kOutput, calls=%fused_computation.21 | convolution fusion | flops 551550976 | bytes 14320128 | tf_op jit(solution)/shard_map/while/body/eval_jaxpr/cond/branch_1_fun/rkgd,ckd->kgrc/dot_general | solution.py:44
  167.5 2.9 fusion.29
  176.3 16.4 %conditional.5 = ((f32[1024,1,4,128]{0,3,2,1:T(8,128)S(1)}, f32[4096,1,128]{2,0,1:T(8,128)}, f32[4096,1,128]{2,0,1:T(8,128)})) conditional(s32[]{:T(128)} %convert_element_type.80, (f32[1024,1,4,128]{0,3,2,1:T(8,128)S(1)}, f32[4096,1,128]{2,0,1:T(8,128)}, f32[4096,1,128]{2,0,1:T(8,128)}) %tuple.100, (bf16[4096,1,128]{2,0,1:T(8,128)(2,1)}, ...), branch_computations={%region_18.18_spmd, %region_19.19_spmd} | conditional | flops 2712338432 | bytes 53409380 | solution.py:29
  179.1 4.4 %fusion.25 = f32[4096,1,128]{2,0,1:T(8,128)} fusion(f32[4096,1,128]{2,0,1:T(8,128)} %get-tuple-element.548, s32[]{:T(128)S(6)} %select_n.47, f32[512,1024,4]{1,0,2:T(8,128)S(1)} %fusion.33, f32[4,1024]{1,0:T(4,128)S(1)} %bitcast.194, pred[1024,512]{0,1:T(8,128)(4,1)S(1)} %compare_and_fusion.1, bf16[1024,1,4,128]{3,0,2,1:T(8,128)(2,1)S(1)} %copy-done.1), kind=kOutput, calls=%fused_computation.31 | convolution fusion | flops 547422208 | bytes 10502148 | tf_op jit(solution)/shard_map/while/body/eval_jaxpr/cond/branch_1_fun/kgrc,rkgd->ckd/dot_general | solution.py:145
  183.5 4.3 %fusion.13 = bf16[4,1024,512]{1,2,0:T(8,128)(2,1)S(1)} fusion(f32[512,1024,4]{1,0,2:T(8,128)S(1)} %fusion.33, f32[4,1024]{1,0:T(4,128)S(1)} %bitcast.197, f32[4,1024]{1,0:T(4,128)S(1)} %bitcast.195, pred[1024,512]{0,1:T(8,128)(4,1)S(1)} %compare_and_fusion.1, bf16[1024,1,4,128]{3,0,2,1:T(8,128)(2,1)S(1)} %copy-done.1, ...), kind=kOutput, calls=%fused_computation.21 | convolution fusion | flops 551550976 | bytes 14320128 | tf_op jit(solution)/shard_map/while/body/eval_jaxpr/cond/branch_1_fun/rkgd,ckd->kgrc/dot_general | solution.py:44
  187.8 2.9 fusion.29
  208.4 16.4 %conditional.5 = ((f32[1024,1,4,128]{0,3,2,1:T(8,128)S(1)}, f32[4096,1,128]{2,0,1:T(8,128)}, f32[4096,1,128]{2,0,1:T(8,128)})) conditional(s32[]{:T(128)} %convert_element_type.80, (f32[1024,1,4,128]{0,3,2,1:T(8,128)S(1)}, f32[4096,1,128]{2,0,1:T(8,128)}, f32[4096,1,128]{2,0,1:T(8,128)}) %tuple.100, (bf16[4096,1,128]{2,0,1:T(8,128)(2,1)}, ...), branch_computations={%region_18.18_spmd, %region_19.19_spmd} | conditional | flops 2712338432 | bytes 53409380 | solution.py:29
  211.2 4.4 %fusion.25 = f32[4096,1,128]{2,0,1:T(8,128)} fusion(f32[4096,1,128]{2,0,1:T(8,128)} %get-tuple-element.548, s32[]{:T(128)S(6)} %select_n.47, f32[512,1024,4]{1,0,2:T(8,128)S(1)} %fusion.33, f32[4,1024]{1,0:T(4,128)S(1)} %bitcast.194, pred[1024,512]{0,1:T(8,128)(4,1)S(1)} %compare_and_fusion.1, bf16[1024,1,4,128]{3,0,2,1:T(8,128)(2,1)S(1)} %copy-done.1), kind=kOutput, calls=%fused_computation.31 | convolution fusion | flops 547422208 | bytes 10502148 | tf_op jit(solution)/shard_map/while/body/eval_jaxpr/cond/branch_1_fun/kgrc,rkgd->ckd/dot_general | solution.py:145
  215.6 4.3 %fusion.13 = bf16[4,1024,512]{1,2,0:T(8,128)(2,1)S(1)} fusion(f32[512,1024,4]{1,0,2:T(8,128)S(1)} %fusion.33, f32[4,1024]{1,0:T(4,128)S(1)} %bitcast.197, f32[4,1024]{1,0:T(4,128)S(1)} %bitcast.195, pred[1024,512]{0,1:T(8,128)(4,1)S(1)} %compare_and_fusion.1, bf16[1024,1,4,128]{3,0,2,1:T(8,128)(2,1)S(1)} %copy-done.1, ...), kind=kOutput, calls=%fused_computation.21 | convolution fusion | flops 551550976 | bytes 14320128 | tf_op jit(solution)/shard_map/while/body/eval_jaxpr/cond/branch_1_fun/rkgd,ckd->kgrc/dot_general | solution.py:44
  219.9 2.9 fusion.29
  234.9 6.0 %all-to-all-start.5 = ((bf16[1024,4,128]{2,1,0:T(4,128)(2,1)}), bf16[1024,4,128]{2,1,0:T(4,128)(2,1)S(1)}, u32[]{:S(2)}, u32[]{:S(2)}) async-start(bf16[1024,4,128]{2,1,0:T(4,128)(2,1)} %bitcast.52), calls=%async_computation.5 | async-start | bytes 2097152 | tf_op jit(solution)/shard_map/all_to_all | solution.py:182
  240.9 46.4 %reduce-scatter.5.cloned.1.call-done = f32[1024,1,128]{2,1,0:T(1,128)} async-done(((f32[4096,1,128]{2,1,0:T(1,128)}), f32[1024,1,128]{2,1,0:T(1,128)}) %reduce-scatter.5.cloned.1.call-update) | async-done | bytes 524304 | tf_op jit(solution)/shard_map/reduce_scatter | solution.py:178
  292.3 5.5 %all-to-all-start.7 = ((bf16[8,2,8192]{2,1,0:T(2,128)(2,1)}), bf16[8,2,8192]{2,1,0:T(2,128)(2,1)S(1)}, u32[]{:S(2)}, u32[]{:S(2)}) async-start(bf16[8,2,8192]{2,1,0:T(2,128)(2,1)} %reshape.167), calls=%async_computation.9 | async-start | bytes 524288 | tf_op jit(solution)/shard_map/all_to_all | solution.py:186
  297.8 23.5 %reduce-scatter.3.cloned.1.call-done = f32[1024,1,128]{2,1,0:T(1,128)} async-done(((f32[4096,1,128]{2,1,0:T(1,128)}), f32[1024,1,128]{2,1,0:T(1,128)}) %reduce-scatter.3.cloned.1.call-update) | async-done | bytes 524304 | tf_op jit(solution)/shard_map/reduce_scatter | solution.py:177
  325.7 5.5 %all-to-all-start.6 = ((bf16[8,2,8192]{2,1,0:T(2,128)(2,1)}), bf16[8,2,8192]{2,1,0:T(2,128)(2,1)S(1)}, u32[]{:S(2)}, u32[]{:S(2)}) async-start(bf16[8,2,8192]{2,1,0:T(2,128)(2,1)} %reshape.165), calls=%async_computation.7 | async-start | bytes 524288 | tf_op jit(solution)/shard_map/all_to_all | solution.py:183
  333.7 6.4 %all-to-all-done.6 = bf16[8,2,8192]{2,1,0:T(2,128)(2,1)S(1)} async-done(((bf16[8,2,8192]{2,1,0:T(2,128)(2,1)}), bf16[8,2,8192]{2,1,0:T(2,128)(2,1)S(1)}, u32[]{:S(2)}, u32[]{:S(2)}) %all-to-all-start.6) | async-done | bytes 262176 | tf_op jit(solution)/shard_map/all_to_all | solution.py:183
  (142 shorter events, 113.7 us)
Async XLA Ops:
  7.2 34.5 %copy-start = (bf16[128,32,128]{2,1,0:T(8,128)(2,1)S(1)}, bf16[128,32,128]{2,1,0:T(8,128)(2,1)}, u32[]{:S(2)}) copy-start(bf16[128,32,128]{2,1,0:T(8,128)(2,1)} %param.19) | copy-start | bytes 3145732
  8.9 16.2 %all-to-all-start = ((bf16[128,8,128]{2,0,1:T(8,128)(2,1)}), bf16[128,8,128]{2,0,1:T(8,128)(2,1)S(1)}, u32[]{:S(2)}, u32[]{:S(2)}) async-start(bf16[128,8,128]{2,0,1:T(8,128)(2,1)} %bitcast.34), calls=%async_computation | async-start | bytes 524288 | tf_op jit(solution)/shard_map/all_to_all | solution.py:75
  25.1 42.1 %copy-start.3 = (bf16[128,8,128]{2,0,1:T(8,128)(2,1)}, bf16[128,8,128]{2,0,1:T(8,128)(2,1)S(1)}, u32[]{:S(2)}) copy-start(bf16[128,8,128]{2,0,1:T(8,128)(2,1)S(1)} %all-to-all-done) | copy-start | bytes 786436
  25.9 12.2 %all-to-all-start.2 = ((bf16[128,8,128]{2,0,1:T(8,128)(2,1)}), bf16[128,8,128]{2,0,1:T(8,128)(2,1)S(1)}, u32[]{:S(2)}, u32[]{:S(2)}) async-start(bf16[128,8,128]{2,0,1:T(8,128)(2,1)} %bitcast.41), calls=%async_computation.2 | async-start | bytes 524288 | tf_op jit(solution)/shard_map/all_to_all | solution.py:76
  29.5 42.0 %copy-start.4 = (s32[4,2]{0,1:T(2,128)S(1)}, s32[4,2]{0,1:T(2,128)}, u32[]{:S(2)}) copy-start(s32[4,2]{0,1:T(2,128)} %param.20) | copy-start | bytes 100
  29.5 42.1 %copy-start.5 = (s32[16]{0:T(128)S(1)}, s32[16]{0:T(128)}, u32[]{:S(2)}) copy-start(s32[16]{0:T(128)} %param.21) | copy-start | bytes 196
  38.1 36.0 %copy-start.2 = (bf16[128,8,128]{2,0,1:T(8,128)(2,1)}, bf16[128,8,128]{2,0,1:T(8,128)(2,1)S(1)}, u32[]{:S(2)}) copy-start(bf16[128,8,128]{2,0,1:T(8,128)(2,1)S(1)} %all-to-all-done.2) | copy-start | bytes 786436
  38.1 29.1 %all-to-all-start.1 = ((bf16[128,32,128]{2,0,1:T(8,128)(2,1)}), bf16[128,32,128]{2,0,1:T(8,128)(2,1)S(1)}, u32[]{:S(2)}, u32[]{:S(2)}) async-start(bf16[128,32,128]{2,0,1:T(8,128)(2,1)} %copy.84), calls=%async_computation.1 | async-start | bytes 2097152 | tf_op jit(solution)/shard_map/all_to_all | solution.py:73
  67.2 29.3 %all-to-all-start.3 = ((bf16[128,32,128]{2,0,1:T(8,128)(2,1)}), bf16[128,32,128]{2,0,1:T(8,128)(2,1)S(1)}, u32[]{:S(2)}, u32[]{:S(2)}) async-start(bf16[128,32,128]{2,0,1:T(8,128)(2,1)} %copy.87), calls=%async_computation.3 | async-start | bytes 2097152 | tf_op jit(solution)/shard_map/all_to_all | solution.py:74
  70.7 30.5 %all-gather.3.cloned.1.call-start = ((), (), s32[]{:S(2)}) async-start(), calls=%async_computation.10 | async-start | bytes 1310720 | tf_op jit(solution)/shard_map/all_gather | solution.py:171
  71.5 77.4 %all-gather.5.cloned.1.call-start = ((), (), s32[]{:S(2)}) async-start(), calls=%async_computation.11 | async-start | bytes 1310720 | tf_op jit(solution)/shard_map/all_gather | solution.py:172
  96.5 52.3 %all-to-all-start.4 = ((f32[128,8,4]{0,2,1:T(4,128)}), f32[128,8,4]{0,2,1:T(4,128)S(1)}, u32[]{:S(2)}, u32[]{:S(2)}) async-start(f32[128,8,4]{0,2,1:T(4,128)} %bitcast.48), calls=%async_computation.4 | async-start | bytes 32768 | tf_op jit(solution)/shard_map/all_to_all | solution.py:78
  100.1 187.1 %reduce-scatter.5.cloned.1.call-start = ((), (), s32[]{:S(2)}) async-start(), calls=%async_computation.13 | async-start | bytes 2621440 | tf_op jit(solution)/shard_map/reduce_scatter | solution.py:178
  156.5 2.3 copy-start.1
  176.8 2.3 copy-start.1
  208.9 2.3 copy-start.1
  232.7 88.5 %reduce-scatter.3.cloned.1.call-start = ((), (), s32[]{:S(2)}) async-start(), calls=%async_computation.12 | async-start | bytes 2621440 | tf_op jit(solution)/shard_map/reduce_scatter | solution.py:177
  234.9 57.3 %all-to-all-start.5 = ((bf16[1024,4,128]{2,1,0:T(4,128)(2,1)}), bf16[1024,4,128]{2,1,0:T(4,128)(2,1)S(1)}, u32[]{:S(2)}, u32[]{:S(2)}) async-start(bf16[1024,4,128]{2,1,0:T(4,128)(2,1)} %bitcast.52), calls=%async_computation.5 | async-start | bytes 2097152 | tf_op jit(solution)/shard_map/all_to_all | solution.py:182
  292.3 33.5 %all-to-all-start.7 = ((bf16[8,2,8192]{2,1,0:T(2,128)(2,1)}), bf16[8,2,8192]{2,1,0:T(2,128)(2,1)S(1)}, u32[]{:S(2)}, u32[]{:S(2)}) async-start(bf16[8,2,8192]{2,1,0:T(2,128)(2,1)} %reshape.167), calls=%async_computation.9 | async-start | bytes 524288 | tf_op jit(solution)/shard_map/all_to_all | solution.py:186
  325.7 14.4 %all-to-all-start.6 = ((bf16[8,2,8192]{2,1,0:T(2,128)(2,1)}), bf16[8,2,8192]{2,1,0:T(2,128)(2,1)S(1)}, u32[]{:S(2)}, u32[]{:S(2)}) async-start(bf16[8,2,8192]{2,1,0:T(2,128)(2,1)} %reshape.165), calls=%async_computation.7 | async-start | bytes 524288 | tf_op jit(solution)/shard_map/all_to_all | solution.py:183
Sparse Core Ops, SparseCore 0:
  73.1 18.0 all-gather.2
  92.8 16.7 all-gather.4
  232.9 54.3 reduce-scatter.4
  289.8 31.4 reduce-scatter.2
where the time goes:
time: 349 us; the launch traced here: 348 us
  waiting for transfers between devices  137 us (39%)
  other arithmetic  72.2 us (21%)
  matrix products  55 us (16%)
  starting transfers between devices  39.1 us (11%)
  local copies, waits for them, and re-layouts  19.8 us (6%)
  between operations  14 us (4%)
  loops' own time  10.8 us (3%)
    reduce_scatter x1, waiting for transfers between devices, shards(): lax.psum_scatter(value_full, 'query', scatter_dimension=0, tiled=True)  46.4 us
    reduce_or x16, other arithmetic, skipping(): jnp.any((pos_query >= jnp.min(pos_key)) & (doc_query >= jnp.min(doc_key))...  40.6 us
    all_to_all x1, waiting for transfers between devices, shards(): lax.all_to_all(queries, 'head', split_axis=1, concat_axis=0, tiled=True)  24.1 us
    reduce_scatter x1, waiting for transfers between devices, shards(): lax.psum_scatter(key_full, 'query', scatter_dimension=0, tiled=True)  23.5 us
    all_to_all x1, waiting for transfers between devices, shards(): lax.all_to_all(out_grad, 'head', split_axis=1, concat_axis=0, tiled=True)  21.6 us
    dot_general x6, matrix products, tile_scores(): jnp.einsum('rkgd,ckd->kgrc', query_tile, key_tile, preferred_element_type...  14.4 us
    dot_general x3, matrix products, compute(): jnp.einsum('kgrc,rkgd->ckd', probability.astype(jnp.bfloat16), grad_here,...  13.2 us
    dot_general x3, matrix products, tile_grads(): jnp.einsum('rkgd,ckd->kgrc', grad_tile, value_tile, preferred_element_typ...  12.8 us
  transfers between devices with their start and end apart: 12, of which 7 were waited for; matrix products, arithmetic and copies ran while one was open for 19% of the time, Pallas kernels for 0%

commit v1 on v0

v1 whole, which is shorter than its diff:
```python
import functools
import math

import jax
import jax.numpy as jnp
from jax import lax
from jax.experimental import pallas as pl
from jax.experimental.pallas import tpu as pltpu
from jax.sharding import PartitionSpec as P

masked = -1e30


def kernel(sizes, order, lengths, kv, query, out_fwd, grad, dquery, dkv, window, cand, picked, prev_out,
           bias, delta, q_rows, g_rows, p_tile, s_tile, partial, sent, came, prev_sum, half_out, half_in,
           back_out, back_in, last_out, last_in, swap_s, swap_r, pick_s, pick_r, prev_s, prev_r, ring_s, ring_r,
           dring_s, dring_r, dprev_s, dprev_r, dpick_s, dpick_r, dswap_s, dswap_r):
    copies, blocks = sizes
    kv_heads, _, rows, width = kv.shape
    group = query.shape[2]
    lanes = rows * group
    keys_seen = (blocks + 1) * rows
    chunk = min(256, lanes)
    token_chunk = chunk // group
    factor = width ** -0.5
    f32, bf16 = jnp.float32, jnp.bfloat16

    mine = lax.axis_index("query")
    head = lax.axis_index("head")
    half, place = lax.div(head, blocks), lax.rem(head, blocks)
    other = 1 - half
    sibling = {"head": other * blocks + place}

    def ahead(d):
        return lax.rem(mine + d, copies)

    def behind(d):
        return lax.rem(mine + (copies - d), copies)

    def lower(t):
        return {"head": half * blocks + lax.rem(place + (blocks - t), blocks)}

    def upper(t):
        return {"head": half * blocks + lax.rem(place + t, blocks)}

    def copy(src, dst, send, recv, to):
        return pltpu.make_async_remote_copy(
            src_ref=src, dst_ref=dst, send_sem=send, recv_sem=recv, device_id=to,
            device_id_type=pl.DeviceIdType.MESH)

    barrier = pltpu.get_barrier_semaphore()
    partners = [sibling]
    partners += [{"query": ahead(d)} for d in range(1, copies)]
    partners += [upper(t) for t in range(1, blocks)]
    for to in partners:
        pl.semaphore_signal(barrier, inc=1, device_id=to, device_id_type=pl.DeviceIdType.MESH)
    pl.semaphore_wait(barrier, len(partners))

    def swap(g):
        return copy(kv.at[g, other], cand.at[g, half], swap_s.at[g], swap_r.at[g], sibling)

    def pick(g, d):
        return copy(picked.at[g, d - 1], cand.at[g, d + 1], pick_s.at[g, d - 1], pick_r.at[g, d - 1],
                    {"query": ahead(d)})

    def prev(g):
        return copy(prev_out.at[g], window.at[g, 0, half], prev_s.at[g], prev_r.at[g], sibling)

    def ring(g, t, own):
        src = kv.at[g] if own else window.at[g, 0]
        return copy(src, window.at[g, t], ring_s.at[g, t - 1], ring_r.at[g, t - 1], lower(t))

    def dring(g, t):
        return copy(sent.at[g, t - 1], came.at[g, t - 1], dring_s.at[g, t - 1], dring_r.at[g, t - 1], upper(t))

    def dprev(g):
        return copy(half_out.at[g], half_in.at[g], dprev_s.at[g], dprev_r.at[g], sibling)

    def dpick(g, d):
        return copy(back_out.at[g, d - 1], back_in.at[g, d - 1], dpick_s.at[g, d - 1], dpick_r.at[g, d - 1],
                    {"query": behind(d)})

    def dswap(g):
        return copy(last_out.at[g], last_in.at[g], dswap_s.at[g], dswap_r.at[g], sibling)

    def each(body):
        def step(g, _):
            body(g)
            return 0
        lax.fori_loop(0, kv_heads, step, 0)

    def source(which):
        wanted = order[mine, which] - 1
        slot = jnp.int32(-1)
        for i in range(2):
            slot = jnp.where(order[mine, i] == wanted, i, slot)
        for d in range(1, copies):
            there = behind(d)
            hit = (order[there, 0] == wanted) | (order[there, 1] == wanted)
            slot = jnp.where(hit, d + 1, slot)
        return slot

    def taken(d):
        there, after = ahead(d), order[mine, 1] + 1
        return (order[there, 0] == after) | (order[there, 1] == after)

    slots = [source(0), source(1)]
    takes = [taken(d) for d in range(1, copies)]

    def first(g):
        swap(g).start()
        for t in range(1, blocks):
            @pl.when(place < t)
            def _():
                ring(g, t, True).start()
    each(first)

    begin = order[mine, half] * (blocks * rows) + place * rows
    row = lax.div(lax.broadcasted_iota(jnp.int32, (1, lanes), 1), jnp.int32(group))
    pos = begin + row

    def bound(i, carry):
        end, low = carry
        end = end + lengths[i]
        return end, jnp.where(pos >= end, end, low)

    _, low = lax.fori_loop(0, lengths.shape[0] - 1, bound, (jnp.int32(0), jnp.zeros_like(pos)))
    low = low - begin + blocks * rows

    def own_and_delta(g):
        cand[g, half] = kv[g, half]
        window[g, blocks] = kv[g]
        product = out_fwd[:, g].astype(f32) * grad[:, g].astype(f32)
        delta[g] = jnp.sum(product.reshape(lanes, width).T, axis=0, keepdims=True)
    each(own_and_delta)

    def choose(g):
        swap(g).wait_recv()
        for d in range(1, copies):
            picked[g, d - 1] = jnp.where(takes[d - 1], cand[g, 1].astype(f32), cand[g, 0].astype(f32)).astype(bf16)
            pick(g, d).start()
    each(choose)

    for c in range(0, lanes, chunk):
        at = lax.broadcasted_iota(jnp.int32, (keys_seen, chunk), 0)
        seen = (at >= low[:, c:c + chunk]) & (at <= row[:, c:c + chunk] + blocks * rows)
        bias[:, c:c + chunk] = jnp.where(seen, 0.0, masked)

    def settle(g):
        for d in range(1, copies):
            pick(g, d).wait_recv()
        both = []
        for i in range(2):
            value = cand[g, 0].astype(f32)
            for k in range(1, copies + 1):
                value = jnp.where(slots[i] == k, cand[g, k].astype(f32), value)
            both.append(value)
        window[g, 0, half] = jnp.where(half == 0, both[0], both[1]).astype(bf16)
        prev_out[g] = jnp.where(half == 0, both[1], both[0]).astype(bf16)
        prev(g).start()
    each(settle)

    def spread(g):
        prev(g).wait_recv()
        for t in range(1, blocks):
            @pl.when(place >= t)
            def _():
                ring(g, t, False).start()
    each(spread)

    def gradients(g):
        for t in range(1, blocks):
            ring(g, t, True).wait_recv()
        q_rows[...] = query[:, g].astype(f32).reshape(lanes, width).astype(bf16)
        g_rows[...] = grad[:, g].astype(f32).reshape(lanes, width).astype(bf16)
        key = window[g, :, 0].reshape(keys_seen, width)
        value = window[g, :, 1].reshape(keys_seen, width)
        key_t = key.astype(f32).T.astype(bf16)
        across = (((1,), (1,)), ((), ()))
        for c in range(0, lanes, chunk):
            cols = slice(c, c + chunk)
            score = lax.dot_general(key, q_rows[cols, :], across, preferred_element_type=f32)
            score = score * (factor * math.log2(math.e)) + bias[:, cols]
            power = jnp.exp2(score - jnp.max(score, axis=0, keepdims=True))
            prob = power * (1.0 / jnp.sum(power, axis=0, keepdims=True))
            grad_prob = lax.dot_general(value, g_rows[cols, :], across, preferred_element_type=f32)
            grad_score = (prob * (grad_prob - delta[g, :, cols])).astype(bf16)
            p_tile[:, cols] = prob.astype(bf16)
            s_tile[:, cols] = grad_score
            dq = jnp.dot(key_t, grad_score, preferred_element_type=f32).T * factor
            first_token = c // group
            dquery[first_token:first_token + token_chunk, g] = dq.reshape(token_chunk, group, width).astype(bf16)
        dk = jnp.dot(s_tile[...], q_rows[...], preferred_element_type=f32) * factor
        dv = jnp.dot(p_tile[...], g_rows[...], preferred_element_type=f32)
        for kind, total in enumerate((dk, dv)):
            total = total.reshape(blocks + 1, rows, width)
            partial[g, 0, kind] = total[0]
            partial[g, 1, kind] = total[blocks]
            sent[g, :, kind] = total[1:blocks].astype(bf16)
        for t in range(1, blocks):
            dring(g, t).start()

    def collect(g):
        earlier, own = partial[g, 0], partial[g, 1]
        for t in range(1, blocks):
            dring(g, t).wait_recv()
            term = came[g, t - 1].astype(f32)
            earlier = earlier + jnp.where(place >= t, term, 0.0)
            own = own + jnp.where(place < t, term, 0.0)
        partial[g, 1] = own
        low_kind = jnp.where(half == 0, earlier[0], earlier[1])
        prev_sum[g] = low_kind.astype(bf16)
        half_out[g] = jnp.where(half == 0, earlier[1], earlier[0]).astype(bf16)
        dprev(g).start()

    def send_back(g):
        dprev(g).wait_recv()
        here, there = prev_sum[g].astype(f32), half_in[g].astype(f32)
        both = [jnp.where(half == 0, here, there), jnp.where(half == 0, there, here)]
        for d in range(1, copies):
            term = jnp.where(slots[0] == d + 1, both[0], 0.0) + jnp.where(slots[1] == d + 1, both[1], 0.0)
            back_out[g, d - 1] = term.astype(bf16)
            dpick(g, d).start()

    def add_up(g):
        here, there = prev_sum[g].astype(f32), half_in[g].astype(f32)
        both = [jnp.where(half == 0, here, there), jnp.where(half == 0, there, here)]
        totals = []
        for i in range(2):
            totals.append(jnp.where(slots[0] == i, both[0], 0.0) + jnp.where(slots[1] == i, both[1], 0.0))
        for d in range(1, copies):
            dpick(g, d).wait_recv()
            term = back_in[g, d - 1].astype(f32)
            totals[1] = totals[1] + jnp.where(takes[d - 1], term, 0.0)
            totals[0] = totals[0] + jnp.where(takes[d - 1], 0.0, term)
        last_out[g] = jnp.where(half == 0, totals[1], totals[0]).astype(bf16)
        partial[g, 0, 0] = jnp.where(half == 0, totals[0], totals[1])
        dswap(g).start()

    def finish(g):
        dswap(g).wait_recv()
        here, there = partial[g, 0, 0], last_in[g].astype(f32)
        dkv[g, 0] = (partial[g, 1, 0] + jnp.where(half == 0, here, there)).astype(bf16)
        dkv[g, 1] = (partial[g, 1, 1] + jnp.where(half == 0, there, here)).astype(bf16)

    chain = (gradients, collect, send_back, add_up, finish)

    def step(s, _):
        for lag, stage in enumerate(chain):
            @pl.when((s >= lag) & (s < kv_heads + lag))
            def _():
                stage(s - lag)
        return 0
    lax.fori_loop(0, kv_heads + len(chain) - 1, step, 0)

    def drain(g):
        for c in (swap(g), prev(g), dprev(g), dswap(g)):
            c.wait_send()
        for d in range(1, copies):
            pick(g, d).wait_send()
            dpick(g, d).wait_send()
        for t in range(1, blocks):
            ring(g, t, True).wait_send()
            dring(g, t).wait_send()
    each(drain)


def shards(copies, blocks, queries, keys, values, attention_out, out_grad, span_order, doc_lengths):
    rows, heads, width = queries.shape
    kv_heads = keys.shape[1]
    group = heads // kv_heads
    lanes, keys_seen = rows * group, (blocks + 1) * rows
    split = (rows, kv_heads, group, width)
    kv = jnp.stack([jnp.transpose(keys, (1, 0, 2)), jnp.transpose(values, (1, 0, 2))], axis=1)
    bf16, f32 = jnp.bfloat16, jnp.float32
    block, pair = (rows, width), (2, rows, width)
    dma = pltpu.SemaphoreType.DMA
    one, over_q, over_j = (kv_heads,), (kv_heads, copies - 1), (kv_heads, blocks - 1)
    vmem, smem = pl.BlockSpec(memory_space=pltpu.VMEM), pl.BlockSpec(memory_space=pltpu.SMEM)
    work = kv_heads * lanes * keys_seen
    dquery, dkv = pl.pallas_call(
        functools.partial(kernel, (copies, blocks)),
        out_shape=(jax.ShapeDtypeStruct(split, bf16), jax.ShapeDtypeStruct(kv.shape, bf16)),
        in_specs=[smem, smem, vmem, vmem, vmem, vmem],
        out_specs=(vmem, vmem),
        scratch_shapes=[
            pltpu.VMEM((kv_heads, blocks + 1) + pair, bf16),
            pltpu.VMEM((kv_heads, copies + 1) + block, bf16),
            pltpu.VMEM(over_q + block, bf16),
            pltpu.VMEM(one + block, bf16),
            pltpu.VMEM((keys_seen, lanes), f32),
            pltpu.VMEM((kv_heads, 1, lanes), f32),
            pltpu.VMEM((lanes, width), bf16),
            pltpu.VMEM((lanes, width), bf16),
            pltpu.VMEM((keys_seen, lanes), bf16),
            pltpu.VMEM((keys_seen, lanes), bf16),
            pltpu.VMEM((kv_heads, 2) + pair, f32),
            pltpu.VMEM(over_j + pair, bf16),
            pltpu.VMEM(over_j + pair, bf16),
            pltpu.VMEM(one + block, bf16),
            pltpu.VMEM(one + block, bf16),
            pltpu.VMEM(one + block, bf16),
            pltpu.VMEM(over_q + block, bf16),
            pltpu.VMEM(over_q + block, bf16),
            pltpu.VMEM(one + block, bf16),
            pltpu.VMEM(one + block, bf16),
            dma(one), dma(one), dma(over_q), dma(over_q), dma(one), dma(one), dma(over_j), dma(over_j),
            dma(over_j), dma(over_j), dma(one), dma(one), dma(over_q), dma(over_q), dma(one), dma(one),
        ],
        compiler_params=pltpu.CompilerParams(
            collective_id=0, has_side_effects=True, vmem_limit_bytes=48 * 1024 * 1024),
        cost_estimate=pl.CostEstimate(
            flops=10 * work * width, bytes_accessed=8 * rows * heads * width, transcendentals=work),
        name="attention_grads",
    )(span_order, doc_lengths, kv, queries.reshape(split), attention_out.reshape(split), out_grad.reshape(split))
    grads = jnp.transpose(dkv, (1, 2, 0, 3))
    return dquery.reshape(queries.shape), grads[0], grads[1]


def solution(mesh):
    spread = P(("query", "head"), None, None)
    return jax.shard_map(
        functools.partial(shards, mesh.shape["query"], mesh.shape["head"] // 2),
        mesh=mesh,
        in_specs=(spread,) * 5 + (P(), P()),
        out_specs=(spread,) * 3,
        check_vma=False,
    )
```

time: 349 us -> 67.8 us (0.19)
  waiting for transfers between devices: 137 us -> 0 us
  other arithmetic: 72.2 us -> 0.03 us
  Pallas kernels: 0 us -> 59.4 us
  matrix products: 55 us -> 0 us
  starting transfers between devices: 39.1 us -> 0 us
  between operations: 14 us -> 0.68 us
  local copies, waits for them, and re-layouts: 19.8 us -> 7.42 us
  loops' own time: 10.8 us -> 0 us
    reduce_scatter x2 -> x0, waiting for transfers between devices: 69.9 us -> none  [the longest x1 46.4 us: shards(): lax.psum_scatter(value_full, 'query', scatter_dimension=0, tiled=True)]
    all_to_all x8 -> x0, waiting for transfers between devices: 66.1 us -> none  [the longest x1 24.1 us: shards(): lax.all_to_all(queries, 'head', split_axis=1, concat_axis=0, tiled=True)]
    pallas_call x0 -> x1, Pallas kernels: none -> 59.4 us  [shards(): pl.pallas_call(functools.partial(kernel, (copies, blocks)), out_shape=(ja...]
    dot_general x18 -> x0, matrix products: 55 us -> none  [the longest x6 14.4 us: tile_scores(): jnp.einsum('rkgd,ckd->kgrc', query_tile, key_tile, preferred_element_type...]
    reduce_or x16 -> x0, other arithmetic: 40.6 us -> none  [skipping(): jnp.any((pos_query >= jnp.min(pos_key)) & (doc_query >= jnp.min(doc_key))...]
    all_to_all x8 -> x0, starting transfers between devices: 38.7 us -> none  [the longest x1 7.28 us: shards(): lax.all_to_all(keys_wide, 'head', split_axis=1, concat_axis=0, tiled=True)]
    reduce_min x16 -> x0, other arithmetic: 12.4 us -> none  [skipping(): jnp.min(doc_key)]
    another operation x18 -> x0, loops' own time: 10.8 us -> none  [the longest x2 10.3 us: blockwise(): return lax.fori_loop(0, length // key_block, advance, totals)]
  transfers between devices with their start and end apart: 12 -> 0, of which waited for: 7 -> 0; matrix products, arithmetic and copies ran while one was open for 19% -> 0% of each run, Pallas kernels for 0% -> 0%
where the time goes in v1:
time: 67.8 us; the launch traced here: 67.5 us
  Pallas kernels  59.4 us (88%)
  local copies, waits for them, and re-layouts  7.42 us (11%)
  between operations  0.68 us (1%)
    pallas_call x1, Pallas kernels, shards(): pl.pallas_call(functools.partial(kernel, (copies, blocks)), out_shape=(ja...  59.4 us
    unnamed x12, local copies, waits for them, and re-layouts  6.4 us

profile of v1, /device:TPU:0, one launch (start us, length us, event | category | flops | bytes accessed | tf_op | source)
XLA Modules:
  0.0 67.5 jit_solution(13828035325812044833)
XLA Ops:
  0.6 0.0 copy-start
  0.6 0.9 %copy.12.order = s32[4,2]{1,0:T(4,128)S(1)} copy(s32[4,2]{0,1:T(2,128)} %param.12) | data formatting | bytes 64 | tf_op args[5]
  1.5 1.0 %copy_bitcast_fusion = (bf16[4,1,128,128]{3,2,1,0:T(8,128)(2,1)S(1)}, bf16[4,1,128,128]{3,2,1,0:T(8,128)(2,1)S(1)}) fusion(bf16[128,4,128]{2,1,0:T(4,128)(2,1)} %param.9, bf16[128,4,128]{2,1,0:T(4,128)(2,1)} %param.8), kind=kLoop, calls=%fused_computation.3 | loop fusion | bytes 524288 | tf_op jit(solution)/shard_map/stack | solution.py:274
  2.5 0.0 copy-start.3
  2.5 0.0 copy-done
  2.6 0.6 copy-done.3
  3.2 0.0 copy-start.1
  3.2 1.2 %copy-done.1 = bf16[128,32,128]{2,1,0:T(8,128)(2,1)S(1)} copy-done((bf16[128,32,128]{2,1,0:T(8,128)(2,1)S(1)}, bf16[128,32,128]{2,1,0:T(8,128)(2,1)}, u32[]{:S(2)}) %copy-start.1) | copy-done | bytes 1048600
  4.4 0.0 copy-start.2
  4.4 1.2 %copy-done.2 = bf16[128,32,128]{2,1,0:T(8,128)(2,1)S(1)} copy-done((bf16[128,32,128]{2,1,0:T(8,128)(2,1)S(1)}, bf16[128,32,128]{2,1,0:T(8,128)(2,1)}, u32[]{:S(2)}) %copy-start.2) | copy-done | bytes 1048600
  5.6 59.4 %attention_grads.1 = (bf16[128,4,8,128]{3,2,1,0:T(8,128)(2,1)S(1)}, bf16[4,2,128,128]{3,2,1,0:T(8,128)(2,1)S(1)}) custom-call(s32[4,2]{1,0:T(4,128)S(1)} %copy.12.order, s32[16]{0:T(128)S(1)} %copy-done.3, bf16[4,2,128,128]{3,2,1,0:T(8,128)(2,1)S(1)} %pad_maximum_fusion.kv, bf16[128,4,8,128]{3,2,1,0:T(8,128)(2,1)S(1)} %bitcast.19, ...), custom_call_target="tpu_custom_call" | custom-call | flops 3355443200 | bytes 4194304 | tf_op jit(solution)/shard_map/attention_grads/pallas_call | solution.py:281
  65.1 0.8 %copy.14 = bf16[128,4,128]{2,1,0:T(4,128)(2,1)} copy(bf16[128,4,128]{2,0,1:T(8,128)(2,1)S(1)} %get-tuple-element.10) | data formatting | bytes 262144
  65.8 0.8 %copy.13 = bf16[128,4,128]{2,1,0:T(4,128)(2,1)} copy(bf16[128,4,128]{2,0,1:T(8,128)(2,1)S(1)} %get-tuple-element.11) | data formatting | bytes 262144
  66.6 1.0 %copy.18 = bf16[128,32,128]{2,1,0:T(8,128)(2,1)} copy(bf16[128,32,128]{2,1,0:T(8,128)(2,1)S(1)} %bitcast.17) | data formatting | bytes 2097152
  (2 shorter events, 0.0 us)
Async XLA Ops:
  0.6 1.9 %copy-start = (bf16[128,32,128]{2,1,0:T(8,128)(2,1)S(1)}, bf16[128,32,128]{2,1,0:T(8,128)(2,1)}, u32[]{:S(2)}) copy-start(bf16[128,32,128]{2,1,0:T(8,128)(2,1)} %param.7) | copy-start | bytes 3145732
  2.5 0.7 copy-start.3
  3.2 1.2 %copy-start.1 = (bf16[128,32,128]{2,1,0:T(8,128)(2,1)S(1)}, bf16[128,32,128]{2,1,0:T(8,128)(2,1)}, u32[]{:S(2)}) copy-start(bf16[128,32,128]{2,1,0:T(8,128)(2,1)} %param.10) | copy-start | bytes 3145732
  4.4 1.2 %copy-start.2 = (bf16[128,32,128]{2,1,0:T(8,128)(2,1)S(1)}, bf16[128,32,128]{2,1,0:T(8,128)(2,1)}, u32[]{:S(2)}) copy-start(bf16[128,32,128]{2,1,0:T(8,128)(2,1)} %param.11) | copy-start | bytes 3145732

commit v2 on v1

v2 whole, which is shorter than its diff:
```python
import functools
import math

import jax
import jax.numpy as jnp
from jax import lax
from jax.experimental import pallas as pl
from jax.experimental.pallas import tpu as pltpu
from jax.sharding import PartitionSpec as P

masked = -1e30


def kernel(sizes, order, lengths, kv, query_far, out_far, grad_far, dquery, dkv, query, out_fwd, grad, window, cand,
           cross_out, cross_in, bias, delta, q_rows, g_rows, p_tile, s_tile, partial, sent, came, half_out, half_in,
           back_out, back_in, load_s, pick_s, pick_r, cross_s, cross_r, ring_s, ring_r,
           dring_s, dring_r, dcross_s, dcross_r, dpick_s, dpick_r):
    copies, blocks = sizes
    kv_heads, _, rows, width = kv.shape
    group = query.shape[2]
    lanes = rows * group
    keys_seen = (blocks + 1) * rows
    chunk = min(256, lanes)
    token_chunk = chunk // group
    factor = width ** -0.5
    f32, bf16 = jnp.float32, jnp.bfloat16

    mine = lax.axis_index("query")
    head = lax.axis_index("head")
    half, place = lax.div(head, blocks), lax.rem(head, blocks)
    other = 1 - half
    sibling = {"head": other * blocks + place}

    def ahead(d):
        return lax.rem(mine + d, copies)

    def behind(d):
        return lax.rem(mine + (copies - d), copies)

    def lower(t):
        return {"head": half * blocks + lax.rem(place + (blocks - t), blocks)}

    def upper(t):
        return {"head": half * blocks + lax.rem(place + t, blocks)}

    def copy(src, dst, send, recv, to):
        return pltpu.make_async_remote_copy(
            src_ref=src, dst_ref=dst, send_sem=send, recv_sem=recv, device_id=to,
            device_id_type=pl.DeviceIdType.MESH)

    loads = [pltpu.make_async_copy(far, near, load_s.at[i]) for i, (far, near) in
             enumerate(((query_far, query), (out_far, out_fwd), (grad_far, grad)))]
    for load in loads:
        load.start()

    barrier = pltpu.get_barrier_semaphore()
    partners = [sibling]
    partners += [{"query": ahead(d)} for d in range(1, copies)]
    partners += [upper(t) for t in range(1, blocks)]
    for to in partners:
        pl.semaphore_signal(barrier, inc=1, device_id=to, device_id_type=pl.DeviceIdType.MESH)
    pl.semaphore_wait(barrier, len(partners))

    def pick(g, d):
        return copy(kv.at[g], cand.at[g, d - 1], pick_s.at[g, d - 1], pick_r.at[g, d - 1], {"query": ahead(d)})

    def cross(g):
        return copy(cross_out.at[g], cross_in.at[g], cross_s.at[g], cross_r.at[g], sibling)

    def ring(g, t, own):
        src = kv.at[g] if own else window.at[g, 0]
        return copy(src, window.at[g, t], ring_s.at[g, t - 1], ring_r.at[g, t - 1], lower(t))

    def dring(g, t):
        return copy(sent.at[g, t - 1], came.at[g, t - 1], dring_s.at[g, t - 1], dring_r.at[g, t - 1], upper(t))

    def dcross(g):
        return copy(half_out.at[g], half_in.at[g], dcross_s.at[g], dcross_r.at[g], sibling)

    def dpick(g, d):
        return copy(back_out.at[g, d - 1], back_in.at[g, d - 1], dpick_s.at[g, d - 1], dpick_r.at[g, d - 1],
                    {"query": behind(d)})

    def each(body):
        def step(g, _):
            body(g)
            return 0
        lax.fori_loop(0, kv_heads, step, 0)

    def source(which):
        wanted = order[mine, which] - 1
        distance, side = jnp.int32(-1), jnp.int32(0)
        for d in range(copies):
            there = behind(d)
            for i in range(2):
                hit = order[there, i] == wanted
                distance, side = jnp.where(hit, d, distance), jnp.where(hit, i, side)
        return distance, side

    far_here, side_here = source(half)
    far_other, side_other = source(other)

    def outgoing(g):
        for d in range(1, copies):
            pick(g, d).start()
    each(outgoing)

    def first(g):
        for t in range(1, blocks):
            @pl.when(place < t)
            def _():
                ring(g, t, True).start()
    each(first)

    begin = order[mine, half] * (blocks * rows) + place * rows
    row = lax.div(lax.broadcasted_iota(jnp.int32, (1, lanes), 1), jnp.int32(group))
    pos = begin + row

    def bound(i, carry):
        end, low = carry
        end = end + lengths[i]
        return end, jnp.where(pos >= end, end, low)

    _, low = lax.fori_loop(0, lengths.shape[0] - 1, bound, (jnp.int32(0), jnp.zeros_like(pos)))
    low = low - begin + blocks * rows

    for c in range(0, lanes, chunk):
        at = lax.broadcasted_iota(jnp.int32, (keys_seen, chunk), 0)
        seen = (at >= low[:, c:c + chunk]) & (at <= row[:, c:c + chunk] + blocks * rows)
        bias[:, c:c + chunk] = jnp.where(seen, 0.0, masked)

    for load in loads:
        load.wait()

    def own_and_delta(g):
        window[g, blocks] = kv[g]
        product = out_fwd[:, g].astype(f32) * grad[:, g].astype(f32)
        delta[g] = jnp.sum(product.reshape(lanes, width).T, axis=0, keepdims=True)

    def exchange(g):
        for d in range(1, copies):
            pick(g, d).wait_recv()
        here = there = kv[g].astype(f32)
        for d in range(1, copies):
            block = cand[g, d - 1].astype(f32)
            here, there = jnp.where(far_here == d, block, here), jnp.where(far_other == d, block, there)
        cross_out[g] = there.astype(bf16)
        cross(g).start()
        window[g, 0] = here.astype(bf16)
        own_and_delta(g)

    def spread(g):
        cross(g).wait_recv()
        window[g, 0] = jnp.where(side_here == half, window[g, 0].astype(f32), cross_in[g].astype(f32)).astype(bf16)
        for t in range(1, blocks):
            @pl.when(place >= t)
            def _():
                ring(g, t, False).start()

    def gradients(g):
        for t in range(1, blocks):
            ring(g, t, True).wait_recv()
        q_rows[...] = query[:, g].astype(f32).reshape(lanes, width).astype(bf16)
        g_rows[...] = grad[:, g].astype(f32).reshape(lanes, width).astype(bf16)
        key = window[g, :, 0].reshape(keys_seen, width)
        value = window[g, :, 1].reshape(keys_seen, width)
        key_t = key.astype(f32).T.astype(bf16)
        across = (((1,), (1,)), ((), ()))
        for c in range(0, lanes, chunk):
            cols = slice(c, c + chunk)
            score = lax.dot_general(key, q_rows[cols, :], across, preferred_element_type=f32)
            score = score * (factor * math.log2(math.e)) + bias[:, cols]
            power = jnp.exp2(score - jnp.max(score, axis=0, keepdims=True))
            prob = power * (1.0 / jnp.sum(power, axis=0, keepdims=True))
            grad_prob = lax.dot_general(value, g_rows[cols, :], across, preferred_element_type=f32)
            grad_score = (prob * (grad_prob - delta[g, :, cols])).astype(bf16)
            p_tile[:, cols] = prob.astype(bf16)
            s_tile[:, cols] = grad_score
            dq = jnp.dot(key_t, grad_score, preferred_element_type=f32).T * factor
            first_token = c // group
            dquery[first_token:first_token + token_chunk, g] = dq.reshape(token_chunk, group, width).astype(bf16)
        dk = jnp.dot(s_tile[...], q_rows[...], preferred_element_type=f32) * factor
        dv = jnp.dot(p_tile[...], g_rows[...], preferred_element_type=f32)
        for kind, total in enumerate((dk, dv)):
            total = total.reshape(blocks + 1, rows, width)
            partial[g, 0, kind] = total[0]
            partial[g, 1, kind] = total[blocks]
            sent[g, :, kind] = total[1:blocks].astype(bf16)
        for t in range(1, blocks):
            dring(g, t).start()

    def collect(g):
        earlier, own = partial[g, 0], partial[g, 1]
        for t in range(1, blocks):
            dring(g, t).wait_recv()
            term = came[g, t - 1].astype(f32)
            earlier = earlier + jnp.where(place >= t, term, 0.0)
            own = own + jnp.where(place < t, term, 0.0)
        partial[g, 0], partial[g, 1] = earlier, own
        half_out[g] = earlier.astype(bf16)
        dcross(g).start()

    def send_back(g):
        dcross(g).wait_recv()
        here, there = partial[g, 0], half_in[g].astype(f32)

        def owed(d):
            return (jnp.where((far_here == d) & (side_here == half), here, 0.0)
                    + jnp.where((far_other == d) & (side_other == half), there, 0.0))

        for d in range(1, copies):
            back_out[g, d - 1] = owed(d).astype(bf16)
            dpick(g, d).start()
        partial[g, 1] = partial[g, 1] + owed(0)

    def finish(g):
        total = partial[g, 1]
        for d in range(1, copies):
            dpick(g, d).wait_recv()
            total = total + back_in[g, d - 1].astype(f32)
        dkv[g] = total.astype(bf16)

    chain = ((0, exchange), (1, spread), (2, gradients), (3, collect), (4, send_back), (5, finish))

    def step(s, _):
        for lag, stage in chain:
            @pl.when((s >= lag) & (s < kv_heads + lag))
            def _():
                stage(s - lag)
        return 0
    lax.fori_loop(0, kv_heads + chain[-1][0], step, 0)

    def drain(g):
        for c in (cross(g), dcross(g)):
            c.wait_send()
        for d in range(1, copies):
            pick(g, d).wait_send()
            dpick(g, d).wait_send()
        for t in range(1, blocks):
            ring(g, t, True).wait_send()
            dring(g, t).wait_send()
    each(drain)


def shards(copies, blocks, queries, keys, values, attention_out, out_grad, span_order, doc_lengths):
    rows, heads, width = queries.shape
    kv_heads = keys.shape[1]
    group = heads // kv_heads
    lanes, keys_seen = rows * group, (blocks + 1) * rows
    split = (rows, kv_heads, group, width)
    kv = jnp.stack([jnp.transpose(keys, (1, 0, 2)), jnp.transpose(values, (1, 0, 2))], axis=1)
    bf16, f32 = jnp.bfloat16, jnp.float32
    pair = (2, rows, width)
    dma = pltpu.SemaphoreType.DMA
    one, over_q, over_j = (kv_heads,), (kv_heads, copies - 1), (kv_heads, blocks - 1)
    vmem, smem = pl.BlockSpec(memory_space=pltpu.VMEM), pl.BlockSpec(memory_space=pltpu.SMEM)
    far = pl.BlockSpec(memory_space=pl.ANY)
    work = kv_heads * lanes * keys_seen
    dquery, dkv = pl.pallas_call(
        functools.partial(kernel, (copies, blocks)),
        out_shape=(jax.ShapeDtypeStruct(split, bf16), jax.ShapeDtypeStruct(kv.shape, bf16)),
        in_specs=[smem, smem, vmem, far, far, far],
        out_specs=(vmem, vmem),
        scratch_shapes=[
            pltpu.VMEM(split, bf16),
            pltpu.VMEM(split, bf16),
            pltpu.VMEM(split, bf16),
            pltpu.VMEM((kv_heads, blocks + 1) + pair, bf16),
            pltpu.VMEM(over_q + pair, bf16),
            pltpu.VMEM(one + pair, bf16),
            pltpu.VMEM(one + pair, bf16),
            pltpu.VMEM((keys_seen, lanes), f32),
            pltpu.VMEM((kv_heads, 1, lanes), f32),
            pltpu.VMEM((lanes, width), bf16),
            pltpu.VMEM((lanes, width), bf16),
            pltpu.VMEM((keys_seen, lanes), bf16),
            pltpu.VMEM((keys_seen, lanes), bf16),
            pltpu.VMEM((kv_heads, 2) + pair, f32),
            pltpu.VMEM(over_j + pair, bf16),
            pltpu.VMEM(over_j + pair, bf16),
            pltpu.VMEM(one + pair, bf16),
            pltpu.VMEM(one + pair, bf16),
            pltpu.VMEM(over_q + pair, bf16),
            pltpu.VMEM(over_q + pair, bf16),
            dma((3,)), dma(over_q), dma(over_q), dma(one), dma(one), dma(over_j), dma(over_j),
            dma(over_j), dma(over_j), dma(one), dma(one), dma(over_q), dma(over_q),
        ],
        compiler_params=pltpu.CompilerParams(
            collective_id=0, has_side_effects=True, vmem_limit_bytes=48 * 1024 * 1024),
        cost_estimate=pl.CostEstimate(
            flops=10 * work * width, bytes_accessed=8 * rows * heads * width, transcendentals=work),
        name="attention_grads",
    )(span_order, doc_lengths, kv, queries.reshape(split), attention_out.reshape(split), out_grad.reshape(split))
    grads = jnp.transpose(dkv, (1, 2, 0, 3))
    return dquery.reshape(queries.shape), grads[0], grads[1]


def solution(mesh):
    spread = P(("query", "head"), None, None)
    return jax.shard_map(
        functools.partial(shards, mesh.shape["query"], mesh.shape["head"] // 2),
        mesh=mesh,
        in_specs=(spread,) * 5 + (P(), P()),
        out_specs=(spread,) * 3,
        check_vma=False,
    )
```

time: 67.8 us -> 64.5 us (0.951); the launches traced: 67.5 us -> 63.3 us
  Pallas kernels: 59.4 us -> 55.1 us
    pallas_call x1, Pallas kernels: 59.4 us -> 55.1 us  [shards(): pl.pallas_call(functools.partial(kernel, (copies, blocks)), out_shape=(ja...]
where the time goes in v2:
time: 64.5 us; the launch traced here: 63.3 us
  Pallas kernels  55.1 us (85%)
  local copies, waits for them, and re-layouts  7.42 us (12%)
  between operations  0.68 us (1%)
    pallas_call x1, Pallas kernels, shards(): pl.pallas_call(functools.partial(kernel, (copies, blocks)), out_shape=(ja...  55.1 us
    unnamed x12, local copies, waits for them, and re-layouts  6.4 us

profile of v2, /device:TPU:0, one launch (start us, length us, event | category | flops | bytes accessed | tf_op | source)
XLA Modules:
  0.0 63.3 jit_solution(12516295794874320932)
XLA Ops:
  0.6 0.0 copy-start
  0.6 0.9 %copy.12.order = s32[4,2]{1,0:T(4,128)S(1)} copy(s32[4,2]{0,1:T(2,128)} %param.12) | data formatting | bytes 64 | tf_op args[5]
  1.5 1.0 %copy_bitcast_fusion = (bf16[4,1,128,128]{3,2,1,0:T(8,128)(2,1)S(1)}, bf16[4,1,128,128]{3,2,1,0:T(8,128)(2,1)S(1)}) fusion(bf16[128,4,128]{2,1,0:T(4,128)(2,1)} %param.9, bf16[128,4,128]{2,1,0:T(4,128)(2,1)} %param.8), kind=kLoop, calls=%fused_computation.3 | loop fusion | bytes 524288 | tf_op jit(solution)/shard_map/stack | solution.py:251
  2.5 0.0 copy-start.3
  2.5 0.0 copy-done
  2.6 0.6 copy-done.3
  3.2 0.0 copy-start.1
  3.2 1.2 %copy-done.1 = bf16[128,32,128]{2,1,0:T(8,128)(2,1)S(1)} copy-done((bf16[128,32,128]{2,1,0:T(8,128)(2,1)S(1)}, bf16[128,32,128]{2,1,0:T(8,128)(2,1)}, u32[]{:S(2)}) %copy-start.1) | copy-done | bytes 1048600
  4.4 0.0 copy-start.2
  4.4 1.2 %copy-done.2 = bf16[128,32,128]{2,1,0:T(8,128)(2,1)S(1)} copy-done((bf16[128,32,128]{2,1,0:T(8,128)(2,1)S(1)}, bf16[128,32,128]{2,1,0:T(8,128)(2,1)}, u32[]{:S(2)}) %copy-start.2) | copy-done | bytes 1048600
  5.6 55.1 %attention_grads.1 = (bf16[128,4,8,128]{3,2,1,0:T(8,128)(2,1)S(1)}, bf16[4,2,128,128]{3,2,1,0:T(8,128)(2,1)S(1)}) custom-call(s32[4,2]{1,0:T(4,128)S(1)} %copy.12.order, s32[16]{0:T(128)S(1)} %copy-done.3, bf16[4,2,128,128]{3,2,1,0:T(8,128)(2,1)S(1)} %pad_maximum_fusion.kv, bf16[128,4,8,128]{3,2,1,0:T(8,128)(2,1)S(1)} %bitcast.19, ...), custom_call_target="tpu_custom_call" | custom-call | flops 3355443200 | bytes 4194304 | tf_op jit(solution)/shard_map/attention_grads/pallas_call | solution.py:259
  60.8 0.8 %copy.14 = bf16[128,4,128]{2,1,0:T(4,128)(2,1)} copy(bf16[128,4,128]{2,0,1:T(8,128)(2,1)S(1)} %get-tuple-element.10) | data formatting | bytes 262144
  61.5 0.8 %copy.13 = bf16[128,4,128]{2,1,0:T(4,128)(2,1)} copy(bf16[128,4,128]{2,0,1:T(8,128)(2,1)S(1)} %get-tuple-element.11) | data formatting | bytes 262144
  62.3 1.0 %copy.18 = bf16[128,32,128]{2,1,0:T(8,128)(2,1)} copy(bf16[128,32,128]{2,1,0:T(8,128)(2,1)S(1)} %bitcast.17) | data formatting | bytes 2097152
  (2 shorter events, 0.0 us)
Async XLA Ops:
  0.6 1.9 %copy-start = (bf16[128,32,128]{2,1,0:T(8,128)(2,1)S(1)}, bf16[128,32,128]{2,1,0:T(8,128)(2,1)}, u32[]{:S(2)}) copy-start(bf16[128,32,128]{2,1,0:T(8,128)(2,1)} %param.7) | copy-start | bytes 3145732
  2.5 0.7 %copy-start.3 = (s32[16]{0:T(128)S(1)}, s32[16]{0:T(128)}, u32[]{:S(2)}) copy-start(s32[16]{0:T(128)} %lengths.1) | copy-start | bytes 196
  3.2 1.2 %copy-start.1 = (bf16[128,32,128]{2,1,0:T(8,128)(2,1)S(1)}, bf16[128,32,128]{2,1,0:T(8,128)(2,1)}, u32[]{:S(2)}) copy-start(bf16[128,32,128]{2,1,0:T(8,128)(2,1)} %param.10) | copy-start | bytes 3145732
  4.4 1.2 %copy-start.2 = (bf16[128,32,128]{2,1,0:T(8,128)(2,1)S(1)}, bf16[128,32,128]{2,1,0:T(8,128)(2,1)}, u32[]{:S(2)}) copy-start(bf16[128,32,128]{2,1,0:T(8,128)(2,1)} %param.11) | copy-start | bytes 3145732
